TPU v7x, 256 devices: a whole 4x4x8 slice. The times are simulated.
256 devices in a mesh: quad: 8 (over z_lo, core), dom: 32 (over x, y, z_hi).
Axes of the slice: x: 4, y: 4, z: 8 (z_hi: 2, z_lo: 4; z = z_hi * 4 + z_lo), core: 2. Of those that a mesh axis runs over, the one named last changes fastest.
Arguments:
- probes: float32 [2, 64, 256, 128], P(None, None, 'dom'), may hold values from -6 to 6
- mass_weights: float32 [256, 128], P('dom'), may hold values from 0.8 to 1.25
- blocks: float32 [2, 256, 128, 128], P(None, 'dom'), may hold values from -4 to 4
- couplings: float32 [2, 6, 256, 128], P(None, None, 'dom'), may hold values from -0.25 to 0.25
Outputs:
- moments: float32 [64, 4, 2, 256, 128], P('quad', None, None, 'dom')
- projected: float32 [2, 8, 64, 64], replicated
All inputs are finite; a program needn't handle non-finite values.
Results may differ from a plain program's by a relative error of at most 0.0001.
Values sent between devices are 32-bit elements; how exact they have to be, the bound alone decides.
A program may use at most 64 MiB of HBM per device.

v0:
```python
import math
import jax
import jax.numpy as jnp
from jax import lax
from jax.sharding import PartitionSpec as P

NQ = 16
ITERS = 4
MOM = 4
PRECISE = lax.Precision.HIGHEST
RADIUS = 2.0
OFFSETS = (-3, -2, -1, 1, 2, 3)


def with_halo(cells, sides, width):
    for axis, dim in sides:
        count = lax.axis_size(axis)
        ends = count - 1
        head = lax.slice_in_dim(cells, 0, width, axis=dim)
        tail = lax.slice_in_dim(cells, cells.shape[dim] - width, cells.shape[dim], axis=dim)
        cells = jnp.concatenate(
            [
                lax.ppermute(tail, axis, [(i, (i + 1) % count) for i in range(ends)]),
                cells,
                lax.ppermute(head, axis, [((i + 1) % count, i) for i in range(ends)]),
            ],
            axis=dim,
        )
    return cells


def shift_angles(shift_index, total_shifts):
    return 2.0 * math.pi / total_shifts * (shift_index.astype(jnp.float32) + 0.5)


def moment_weights(angles, moment_count, scale):
    orders = jnp.arange(1, moment_count + 1, dtype=jnp.float32)
    phases = orders[:, None] * angles[None, :]
    return (scale * jnp.cos(phases), scale * jnp.sin(phases))


def sweep(field, padded, blocks, couplings, zmass_re, zmass_im, inverse_re, inverse_im, source):
    rim_depth = max(OFFSETS)
    line_count = field.shape[3]
    field_re = field[0]
    field_im = field[1]
    image_re = jnp.einsum("spxj,xij->spxi", field_re, blocks[0], precision=PRECISE) - jnp.einsum(
        "spxj,xij->spxi", field_im, blocks[1], precision=PRECISE
    )
    image_im = jnp.einsum("spxj,xij->spxi", field_im, blocks[0], precision=PRECISE) + jnp.einsum(
        "spxj,xij->spxi", field_re, blocks[1], precision=PRECISE
    )
    for position, offset in enumerate(OFFSETS):
        neighbour = padded[:, :, :, rim_depth + offset : rim_depth + offset + line_count]
        coup_re = couplings[0, position]
        coup_im = couplings[1, position]
        image_re = image_re + coup_re * neighbour[0] - coup_im * neighbour[1]
        image_im = image_im + coup_re * neighbour[1] + coup_im * neighbour[0]
    resid_re = source[0] - (zmass_re * field_re - zmass_im * field_im) + image_re
    resid_im = source[1] - (zmass_re * field_im + zmass_im * field_re) + image_im
    return jnp.stack(
        [
            field_re + resid_re * inverse_re - resid_im * inverse_im,
            field_im + resid_re * inverse_im + resid_im * inverse_re,
        ]
    )


def moment_block(field_part, weight_re, weight_im):
    sum_re = jnp.einsum("ks,spxi->pkxi", weight_re, field_part[0], precision=PRECISE) - jnp.einsum(
        "ks,spxi->pkxi", weight_im, field_part[1], precision=PRECISE
    )
    sum_im = jnp.einsum("ks,spxi->pkxi", weight_re, field_part[1], precision=PRECISE) + jnp.einsum(
        "ks,spxi->pkxi", weight_im, field_part[0], precision=PRECISE
    )
    return jnp.stack([sum_re, sum_im], axis=2)


def project(gram_re, gram_im, angles, scale):
    proj_re, proj_im = moment_weights(angles, 2 * MOM, scale)
    mixed_re = jnp.einsum("ks,spq->kpq", proj_re, gram_re, precision=PRECISE) - jnp.einsum(
        "ks,spq->kpq", proj_im, gram_im, precision=PRECISE
    )
    mixed_im = jnp.einsum("ks,spq->kpq", proj_re, gram_im, precision=PRECISE) + jnp.einsum(
        "ks,spq->kpq", proj_im, gram_re, precision=PRECISE
    )
    return jnp.stack([mixed_re, mixed_im])


def on_device(probes, mass_weights, blocks, couplings):
    rim_depth = max(OFFSETS)
    shift_count = NQ // lax.axis_size("quad")
    probe_count = probes.shape[1]
    owned_probes = probe_count // lax.axis_size("quad")
    line_count = probes.shape[2]
    row_width = probes.shape[3]
    total_lines = line_count * lax.axis_size("dom")
    shift_index = lax.axis_index("quad") * shift_count + jnp.arange(shift_count, dtype=jnp.int32)
    angles = shift_angles(shift_index, NQ)
    zmass_re = (RADIUS * jnp.cos(angles))[:, None, None, None] * mass_weights[None, None]
    zmass_im = (RADIUS * jnp.sin(angles))[:, None, None, None] * mass_weights[None, None]
    diagonal = jnp.diagonal(blocks, axis1=2, axis2=3)
    denom_re = zmass_re - diagonal[0]
    denom_im = zmass_im - diagonal[1]
    modulus = denom_re * denom_re + denom_im * denom_im
    inverse_re = denom_re / modulus
    inverse_im = -denom_im / modulus
    source = mass_weights[None, None] * probes
    field = jnp.stack(
        [
            source[0] * inverse_re - source[1] * inverse_im,
            source[0] * inverse_im + source[1] * inverse_re,
        ]
    )
    for step in range(ITERS - 1):
        padded = with_halo(field, (("dom", 3),), rim_depth)
        field = sweep(
            field, padded, blocks, couplings, zmass_re, zmass_im, inverse_re, inverse_im, source
        )
    weight_re, weight_im = moment_weights(angles, MOM, RADIUS / NQ)
    field_rows = lax.slice_in_dim(field, 0, owned_probes * lax.axis_size("quad"), axis=2)
    moments = lax.psum_scatter(
        moment_block(field_rows, weight_re, weight_im), "quad", scatter_dimension=0, tiled=True
    )
    gram_re = jnp.einsum("pxi,sqxi->spq", probes[0], field[0], precision=PRECISE) + jnp.einsum(
        "pxi,sqxi->spq", probes[1], field[1], precision=PRECISE
    )
    gram_im = jnp.einsum("pxi,sqxi->spq", probes[0], field[1], precision=PRECISE) - jnp.einsum(
        "pxi,sqxi->spq", probes[1], field[0], precision=PRECISE
    )
    scale = RADIUS / (NQ * total_lines * row_width)
    projected = lax.psum(project(gram_re, gram_im, angles, scale), ("quad", "dom"))
    return (moments, projected)


def solution(mesh):
    return jax.shard_map(
        on_device,
        mesh=mesh,
        in_specs=(
            P(None, None, "dom", None),
            P("dom", None),
            P(None, "dom", None, None),
            P(None, None, "dom", None),
        ),
        out_specs=(P("quad", None, None, "dom", None), P()),
        check_vma=False,
    )
```

profile of v0, /device:TPU:2, one launch (start us, length us, event | category | flops | bytes accessed | tf_op | source)
XLA Modules:
  0.0 444.9 jit_solution(10704677841827037540)
XLA Ops:
  8.0 0.0 all-reduce.2.cloned.1.call-start
  8.1 0.0 copy-start.3
  8.1 13.3 %copy.50 = f32[2,8,128,128]{1,0,3,2:T(2,128)} copy(f32[2,8,128,128]{3,2,1,0:T(8,128)} %param.6) | data formatting | bytes 2097152 | tf_op args[2]
  21.3 6.7 %gather_fusion = f32[128,2,8]{2,1,0:T(2,128)S(1)} fusion(f32[2,8,128,128]{1,0,3,2:T(2,128)} %copy.50, s32[128]{0:T(128)S(1)} %or_bitcast_fusion), kind=kCustom, calls=%fused_computation | custom fusion | bytes 17408 | tf_op jit(solution)/shard_map/jit(diagonal)/gather | solution.py:102
  28.0 0.1 fusion.130
  28.2 0.1 copy.51
  28.3 0.1 sine_multiply_fusion
  28.4 0.1 copy.53
  28.5 0.1 copy.49
  28.6 0.1 fusion.78
  28.7 0.0 copy-start
  28.7 0.2 multiply_subtract_fusion.3
  28.8 0.1 pad_maximum_fusion.9
  28.9 11.7 %collective-permute-start.1 = (f32[2,2,64,3,128]{4,2,1,3,0:T(8,128)S(1)}, f32[2,2,64,3,128]{4,2,1,3,0:T(8,128)S(1)}, u32[]{:S(2)}, u32[]{:S(2)}) collective-permute-start(f32[2,2,64,3,128]{4,2,1,3,0:T(8,128)S(1)} %get-tuple-element.24), channel_id=1, source_target_pairs={{1,0},{2,1},{3,2},{4,3},{5,4},{6,5},{7,6},{8,7},{9,8},{10,9},{11,1... | collective-permute-start | bytes 1179656 | tf_op jit(solution)/shard_map/ppermute | solution.py:25
  40.6 1.9 collective-permute-start
  42.5 1.2 fusion.30
  43.9 1.2 fusion.28
  45.1 7.2 %collective-permute-done.1 = f32[2,2,64,3,128]{4,2,1,3,0:T(8,128)S(1)} collective-permute-done((f32[2,2,64,3,128]{4,2,1,3,0:T(8,128)S(1)}, f32[2,2,64,3,128]{4,2,1,3,0:T(8,128)S(1)}, u32[]{:S(2)}, u32[]{:S(2)}) %collective-permute-start.1) | collective-permute-done | bytes 393248 | tf_op jit(solution)/shard_map/ppermute | solution.py:25
  52.3 21.3 %collective-permute-done = f32[2,2,64,3,128]{4,2,1,3,0:T(8,128)S(1)} collective-permute-done((f32[2,2,64,3,128]{4,2,1,3,0:T(8,128)S(1)}, f32[2,2,64,3,128]{4,2,1,3,0:T(8,128)S(1)}, u32[]{:S(2)}, u32[]{:S(2)}) %collective-permute-start) | collective-permute-done | bytes 393248 | tf_op jit(solution)/shard_map/ppermute | solution.py:23
  73.6 0.4 pad_maximum_fusion.1
  74.0 1.9 subtract_add_fusion.2
  75.9 2.2 multiply_add_fusion.2
  78.1 0.1 pad_maximum_fusion.7
  78.2 8.9 %collective-permute-start.3 = (f32[2,2,64,3,128]{4,2,1,3,0:T(8,128)S(1)}, f32[2,2,64,3,128]{4,2,1,3,0:T(8,128)S(1)}, u32[]{:S(2)}, u32[]{:S(2)}) collective-permute-start(f32[2,2,64,3,128]{4,2,1,3,0:T(8,128)S(1)} %get-tuple-element.20), channel_id=1, source_target_pairs={{1,0},{2,1},{3,2},{4,3},{5,4},{6,5},{7,6},{8,7},{9,8},{10,9},{11,1... | collective-permute-start | bytes 1179656 | tf_op jit(solution)/shard_map/ppermute | solution.py:25
  87.1 1.9 collective-permute-start.2
  89.0 1.2 fusion.26
  90.3 1.2 fusion.24
  91.5 12.3 %collective-permute-done.3 = f32[2,2,64,3,128]{4,2,1,3,0:T(8,128)S(1)} collective-permute-done((f32[2,2,64,3,128]{4,2,1,3,0:T(8,128)S(1)}, f32[2,2,64,3,128]{4,2,1,3,0:T(8,128)S(1)}, u32[]{:S(2)}, u32[]{:S(2)}) %collective-permute-start.3) | collective-permute-done | bytes 393248 | tf_op jit(solution)/shard_map/ppermute | solution.py:25
  103.8 8.8 %collective-permute-done.2 = f32[2,2,64,3,128]{4,2,1,3,0:T(8,128)S(1)} collective-permute-done((f32[2,2,64,3,128]{4,2,1,3,0:T(8,128)S(1)}, f32[2,2,64,3,128]{4,2,1,3,0:T(8,128)S(1)}, u32[]{:S(2)}, u32[]{:S(2)}) %collective-permute-start.2) | collective-permute-done | bytes 393248 | tf_op jit(solution)/shard_map/ppermute | solution.py:23
  112.6 0.4 pad_maximum_fusion.2
  112.9 1.8 subtract_add_fusion.1
  114.8 2.1 multiply_add_fusion.1
  116.8 0.1 pad_maximum_fusion.5
  116.9 7.4 %collective-permute-start.5 = (f32[2,2,64,3,128]{4,2,1,3,0:T(8,128)S(1)}, f32[2,2,64,3,128]{4,2,1,3,0:T(8,128)S(1)}, u32[]{:S(2)}, u32[]{:S(2)}) collective-permute-start(f32[2,2,64,3,128]{4,2,1,3,0:T(8,128)S(1)} %get-tuple-element.16), channel_id=1, source_target_pairs={{1,0},{2,1},{3,2},{4,3},{5,4},{6,5},{7,6},{8,7},{9,8},{10,9},{11,1... | collective-permute-start | bytes 1179656 | tf_op jit(solution)/shard_map/ppermute | solution.py:25
  124.3 3.7 collective-permute-start.4
  128.1 1.2 fusion.22
  129.3 1.2 fusion.20
  130.5 1.3 collective-permute-done.5
  131.8 22.8 %collective-permute-done.4 = f32[2,2,64,3,128]{4,2,1,3,0:T(8,128)S(1)} collective-permute-done((f32[2,2,64,3,128]{4,2,1,3,0:T(8,128)S(1)}, f32[2,2,64,3,128]{4,2,1,3,0:T(8,128)S(1)}, u32[]{:S(2)}, u32[]{:S(2)}) %collective-permute-start.4) | collective-permute-done | bytes 393248 | tf_op jit(solution)/shard_map/ppermute | solution.py:23
  154.6 0.3 pad_maximum_fusion.3
  154.8 1.9 subtract_add_fusion
  156.8 2.1 multiply_subtract_fusion
  158.8 2.2 fusion.36
  161.0 2.2 fusion.40
  163.2 0.6 convolution_bitcast_fusion
  163.8 0.6 convolution_bitcast_fusion.2
  164.4 2.5 fusion
  166.9 2.3 fusion.1
  169.2 0.6 fusion.13
  169.8 0.1 copy.64
  169.9 0.6 fusion.11
  170.5 0.1 copy.63
  170.6 0.5 fusion.89
  171.1 0.5 fusion.91
  171.7 0.5 fusion.9
  172.2 0.5 fusion.8
  172.7 0.8 pad_maximum_fusion.4
  173.6 0.0 all-reduce.2.cloned.1.call-update
  173.6 0.0 reduce-scatter.2.cloned.1.call-start
  173.7 0.5 pad_maximum_fusion
  174.2 1.5 copy.60
  175.7 0.0 reduce-scatter.2.cloned.1.call-update
  175.8 259.7 %all-reduce.2.cloned.1.call-done = f32[2,8,64,64]{3,1,2,0:T(8,128)} async-done(((f32[2,8,64,64]{3,1,2,0:T(8,128)}), f32[2,8,64,64]{3,1,2,0:T(8,128)}) %all-reduce.2.cloned.1.call-update) | async-done | bytes 262160 | tf_op jit(solution)/shard_map/psum | solution.py:132
  435.5 1.9 copy.67
  (16 shorter events, 0.2 us)
Async XLA Ops:
  8.0 427.5 %all-reduce.2.cloned.1.call-start = ((), (), s32[]{:S(2)}) async-start(), calls=%async_computation.2 | async-start | bytes 1048576 | tf_op jit(solution)/shard_map/psum | solution.py:132
  8.1 20.3 %copy-start.1 = (f32[2,64,8,128]{3,2,1,0:T(8,128)S(1)}, f32[2,64,8,128]{3,2,1,0:T(8,128)}, u32[]{:S(2)}) copy-start(f32[2,64,8,128]{3,2,1,0:T(8,128)} %param.4) | copy-start | bytes 1572868
  8.1 20.3 %copy-start.3 = (f32[8,128]{1,0:T(8,128)S(1)}, f32[8,128]{1,0:T(8,128)}, u32[]{:S(2)}) copy-start(f32[8,128]{1,0:T(8,128)} %param.5) | copy-start | bytes 12292
  28.7 13.9 %copy-start = (f32[2,8,128,128]{3,2,1,0:T(8,128)S(1)}, f32[2,8,128,128]{3,2,1,0:T(8,128)}, u32[]{:S(2)}) copy-start(f32[2,8,128,128]{3,2,1,0:T(8,128)} %param.6) | copy-start | bytes 3145732
  28.9 14.9 %copy-start.2 = (f32[2,6,8,128]{3,2,1,0:T(8,128)S(1)}, f32[2,6,8,128]{3,2,1,0:T(8,128)}, u32[]{:S(2)}) copy-start(f32[2,6,8,128]{3,2,1,0:T(8,128)} %param.7) | copy-start | bytes 147460
  28.9 23.3 %collective-permute-start.1 = (f32[2,2,64,3,128]{4,2,1,3,0:T(8,128)S(1)}, f32[2,2,64,3,128]{4,2,1,3,0:T(8,128)S(1)}, u32[]{:S(2)}, u32[]{:S(2)}) collective-permute-start(f32[2,2,64,3,128]{4,2,1,3,0:T(8,128)S(1)} %get-tuple-element.24), channel_id=1, source_target_pairs={{1,0},{2,1},{3,2},{4,3},{5,4},{6,5},{7,6},{8,7},{9,8},{10,9},{11,1... | collective-permute-start | bytes 1179656 | tf_op jit(solution)/shard_map/ppermute | solution.py:25
  40.6 33.0 %collective-permute-start = (f32[2,2,64,3,128]{4,2,1,3,0:T(8,128)S(1)}, f32[2,2,64,3,128]{4,2,1,3,0:T(8,128)S(1)}, u32[]{:S(2)}, u32[]{:S(2)}) collective-permute-start(f32[2,2,64,3,128]{4,2,1,3,0:T(8,128)S(1)} %get-tuple-element.25), channel_id=1, source_target_pairs={{0,1},{1,2},{2,3},{3,4},{4,5},{5,6},{6,7},{7,8},{8,9},{9,10},{10,1... | collective-permute-start | bytes 1179656 | tf_op jit(solution)/shard_map/ppermute | solution.py:23
  78.2 25.6 %collective-permute-start.3 = (f32[2,2,64,3,128]{4,2,1,3,0:T(8,128)S(1)}, f32[2,2,64,3,128]{4,2,1,3,0:T(8,128)S(1)}, u32[]{:S(2)}, u32[]{:S(2)}) collective-permute-start(f32[2,2,64,3,128]{4,2,1,3,0:T(8,128)S(1)} %get-tuple-element.20), channel_id=1, source_target_pairs={{1,0},{2,1},{3,2},{4,3},{5,4},{6,5},{7,6},{8,7},{9,8},{10,9},{11,1... | collective-permute-start | bytes 1179656 | tf_op jit(solution)/shard_map/ppermute | solution.py:25
  87.1 25.5 %collective-permute-start.2 = (f32[2,2,64,3,128]{4,2,1,3,0:T(8,128)S(1)}, f32[2,2,64,3,128]{4,2,1,3,0:T(8,128)S(1)}, u32[]{:S(2)}, u32[]{:S(2)}) collective-permute-start(f32[2,2,64,3,128]{4,2,1,3,0:T(8,128)S(1)} %get-tuple-element.21), channel_id=1, source_target_pairs={{0,1},{1,2},{2,3},{3,4},{4,5},{5,6},{6,7},{7,8},{8,9},{9,10},{10,1... | collective-permute-start | bytes 1179656 | tf_op jit(solution)/shard_map/ppermute | solution.py:23
  116.9 14.9 %collective-permute-start.5 = (f32[2,2,64,3,128]{4,2,1,3,0:T(8,128)S(1)}, f32[2,2,64,3,128]{4,2,1,3,0:T(8,128)S(1)}, u32[]{:S(2)}, u32[]{:S(2)}) collective-permute-start(f32[2,2,64,3,128]{4,2,1,3,0:T(8,128)S(1)} %get-tuple-element.16), channel_id=1, source_target_pairs={{1,0},{2,1},{3,2},{4,3},{5,4},{6,5},{7,6},{8,7},{9,8},{10,9},{11,1... | collective-permute-start | bytes 1179656 | tf_op jit(solution)/shard_map/ppermute | solution.py:25
  124.3 30.2 %collective-permute-start.4 = (f32[2,2,64,3,128]{4,2,1,3,0:T(8,128)S(1)}, f32[2,2,64,3,128]{4,2,1,3,0:T(8,128)S(1)}, u32[]{:S(2)}, u32[]{:S(2)}) collective-permute-start(f32[2,2,64,3,128]{4,2,1,3,0:T(8,128)S(1)} %get-tuple-element.17), channel_id=1, source_target_pairs={{0,1},{1,2},{2,3},{3,4},{4,5},{5,6},{6,7},{7,8},{8,9},{9,10},{10,1... | collective-permute-start | bytes 1179656 | tf_op jit(solution)/shard_map/ppermute | solution.py:23
  173.6 263.8 %reduce-scatter.2.cloned.1.call-start = ((), (), s32[]{:S(2)}) async-start(), calls=%async_computation.1 | async-start | bytes 2359296 | tf_op jit(solution)/shard_map/reduce_scatter | solution.py:122
Sparse Core Ops, SparseCore 0:
  173.7 261.7 all-reduce.1
Sparse Core Ops, SparseCore 1:
  177.2 49.0 reduce-scatter.1
where the time goes:
time: 446 us; the launch traced here: 445 us
  waiting for transfers between devices  333 us (75%)
  starting transfers between devices  35.6 us (8%)
  matrix products  32.9 us (7%)
  local copies, waits for them, and re-layouts  24 us (5%)
  between operations  15.9 us (4%)
    psum x1, waiting for transfers between devices, on_device(): lax.psum(project(gram_re, gram_im, angles, scale), ('quad', 'dom'))  260 us
    ppermute x3, waiting for transfers between devices, with_halo(): lax.ppermute(tail, axis, [(i, (i + 1) % count) for i in range(ends)])  52.9 us
    ppermute x3, starting transfers between devices, with_halo(): lax.ppermute(head, axis, [((i + 1) % count, i) for i in range(ends)])  28 us
    ppermute x3, waiting for transfers between devices, with_halo(): lax.ppermute(head, axis, [((i + 1) % count, i) for i in range(ends)])  20.8 us
    unnamed x10, local copies, waits for them, and re-layouts  15.2 us
  transfers between devices with their start and end apart: 8, of which 7 were waited for; matrix products, arithmetic and copies ran while one was open for 3% of the time, Pallas kernels for 0%

commit v1 on v0

--- a/solution.py
+++ b/solution.py
@@ -129,7 +129,7 @@
         "pxi,sqxi->spq", probes[1], field[0], precision=PRECISE
     )
     scale = RADIUS / (NQ * total_lines * row_width)
-    projected = lax.psum(project(gram_re, gram_im, angles, scale), ("quad", "dom"))
+    projected = lax.psum(lax.psum(project(gram_re, gram_im, angles, scale), "dom"), "quad")
     return (moments, projected)
 
 

time: 446 us -> 727 us (1.63)
  waiting for transfers between devices: 333 us -> 617 us
    psum x1 -> x2, waiting for transfers between devices: 260 us -> 502 us  [the longest x1 427 us: on_device(): lax.psum(project(gram_re, gram_im, angles, scale), 'dom')]
    reduce_scatter x1, waiting for transfers between devices: 0.01 us -> 41.3 us  [on_device(): lax.psum_scatter(moment_block(field_rows, weight_re, weight_im), 'quad',...]
  transfers between devices with their start and end apart: 8 -> 9, of which waited for: 7 -> 9; matrix products, arithmetic and copies ran while one was open for 3% -> 2% of each run, Pallas kernels for 0% -> 0%
where the time goes in v1:
time: 727 us; the launch traced here: 726 us
  waiting for transfers between devices  617 us (85%)
  starting transfers between devices  35.8 us (5%)
  matrix products  32.7 us (4%)
  local copies, waits for them, and re-layouts  24 us (3%)
  between operations  14.2 us (2%)
    psum x1, waiting for transfers between devices, on_device(): lax.psum(project(gram_re, gram_im, angles, scale), 'dom')  427 us
    psum x1, waiting for transfers between devices, on_device(): lax.psum(lax.psum(project(gram_re, gram_im, angles, scale), 'dom'), 'quad')  74.4 us
    ppermute x3, waiting for transfers between devices, with_halo(): lax.ppermute(tail, axis, [(i, (i + 1) % count) for i in range(ends)])  52.1 us
    reduce_scatter x1, waiting for transfers between devices, on_device(): lax.psum_scatter(moment_block(field_rows, weight_re, weight_im), 'quad',...  41.3 us
    ppermute x3, starting transfers between devices, with_halo(): lax.ppermute(head, axis, [((i + 1) % count, i) for i in range(ends)])  28 us
    ppermute x3, waiting for transfers between devices, with_halo(): lax.ppermute(head, axis, [((i + 1) % count, i) for i in range(ends)])  21.4 us
    unnamed x10, local copies, waits for them, and re-layouts  15.2 us
  transfers between devices with their start and end apart: 9, of which 9 were waited for; matrix products, arithmetic and copies ran while one was open for 2% of the time, Pallas kernels for 0%

profile of v1, /device:TPU:2, one launch (start us, length us, event | category | flops | bytes accessed | tf_op | source)
XLA Modules:
  0.0 726.2 jit_solution(16526051203622561968)
XLA Ops:
  7.2 0.0 all-reduce.3.cloned.1.call-start
  7.2 13.3 %copy.50 = f32[2,8,128,128]{1,0,3,2:T(2,128)} copy(f32[2,8,128,128]{3,2,1,0:T(8,128)} %param.6) | data formatting | bytes 2097152 | tf_op args[2]
  20.5 6.7 gather_fusion
  27.2 0.1 fusion.130
  27.4 0.1 copy.51
  27.4 0.1 sine_multiply_fusion
  27.6 0.1 copy.53
  27.7 0.1 copy.49
  27.7 0.1 fusion.78
  27.8 0.1 multiply_subtract_fusion.3
  28.0 0.1 pad_maximum_fusion.9
  28.1 11.7 %collective-permute-start.1 = (f32[2,2,64,3,128]{4,2,1,3,0:T(8,128)S(1)}, f32[2,2,64,3,128]{4,2,1,3,0:T(8,128)S(1)}, u32[]{:S(2)}, u32[]{:S(2)}) collective-permute-start(f32[2,2,64,3,128]{4,2,1,3,0:T(8,128)S(1)} %get-tuple-element.24), channel_id=1, source_target_pairs={{1,0},{2,1},{3,2},{4,3},{5,4},{6,5},{7,6},{8,7},{9,8},{10,9},{11,1... | collective-permute-start | bytes 1179656 | tf_op jit(solution)/shard_map/ppermute | solution.py:25
  39.7 1.9 collective-permute-start
  41.7 1.2 fusion.30
  43.0 1.2 fusion.28
  44.2 7.2 collective-permute-done.1
  51.4 21.3 %collective-permute-done = f32[2,2,64,3,128]{4,2,1,3,0:T(8,128)S(1)} collective-permute-done((f32[2,2,64,3,128]{4,2,1,3,0:T(8,128)S(1)}, f32[2,2,64,3,128]{4,2,1,3,0:T(8,128)S(1)}, u32[]{:S(2)}, u32[]{:S(2)}) %collective-permute-start) | collective-permute-done | bytes 393248 | tf_op jit(solution)/shard_map/ppermute | solution.py:23
  72.7 0.4 pad_maximum_fusion.1
  73.1 1.9 subtract_add_fusion.2
  75.0 2.2 multiply_add_fusion.2
  77.2 0.1 pad_maximum_fusion.7
  77.3 8.9 %collective-permute-start.3 = (f32[2,2,64,3,128]{4,2,1,3,0:T(8,128)S(1)}, f32[2,2,64,3,128]{4,2,1,3,0:T(8,128)S(1)}, u32[]{:S(2)}, u32[]{:S(2)}) collective-permute-start(f32[2,2,64,3,128]{4,2,1,3,0:T(8,128)S(1)} %get-tuple-element.20), channel_id=1, source_target_pairs={{1,0},{2,1},{3,2},{4,3},{5,4},{6,5},{7,6},{8,7},{9,8},{10,9},{11,1... | collective-permute-start | bytes 1179656 | tf_op jit(solution)/shard_map/ppermute | solution.py:25
  86.2 1.9 collective-permute-start.2
  88.2 1.2 fusion.26
  89.4 1.2 fusion.24
  90.6 12.9 %collective-permute-done.3 = f32[2,2,64,3,128]{4,2,1,3,0:T(8,128)S(1)} collective-permute-done((f32[2,2,64,3,128]{4,2,1,3,0:T(8,128)S(1)}, f32[2,2,64,3,128]{4,2,1,3,0:T(8,128)S(1)}, u32[]{:S(2)}, u32[]{:S(2)}) %collective-permute-start.3) | collective-permute-done | bytes 393248 | tf_op jit(solution)/shard_map/ppermute | solution.py:25
  103.5 8.1 %collective-permute-done.2 = f32[2,2,64,3,128]{4,2,1,3,0:T(8,128)S(1)} collective-permute-done((f32[2,2,64,3,128]{4,2,1,3,0:T(8,128)S(1)}, f32[2,2,64,3,128]{4,2,1,3,0:T(8,128)S(1)}, u32[]{:S(2)}, u32[]{:S(2)}) %collective-permute-start.2) | collective-permute-done | bytes 393248 | tf_op jit(solution)/shard_map/ppermute | solution.py:23
  111.6 0.4 pad_maximum_fusion.2
  112.0 1.8 subtract_add_fusion.1
  113.8 2.0 multiply_add_fusion.1
  115.8 0.1 pad_maximum_fusion.5
  115.9 7.5 %collective-permute-start.5 = (f32[2,2,64,3,128]{4,2,1,3,0:T(8,128)S(1)}, f32[2,2,64,3,128]{4,2,1,3,0:T(8,128)S(1)}, u32[]{:S(2)}, u32[]{:S(2)}) collective-permute-start(f32[2,2,64,3,128]{4,2,1,3,0:T(8,128)S(1)} %get-tuple-element.16), channel_id=1, source_target_pairs={{1,0},{2,1},{3,2},{4,3},{5,4},{6,5},{7,6},{8,7},{9,8},{10,9},{11,1... | collective-permute-start | bytes 1179656 | tf_op jit(solution)/shard_map/ppermute | solution.py:25
  123.3 3.8 collective-permute-start.4
  127.1 1.2 fusion.22
  128.3 1.2 fusion.20
  129.6 1.3 collective-permute-done.5
  130.9 22.7 %collective-permute-done.4 = f32[2,2,64,3,128]{4,2,1,3,0:T(8,128)S(1)} collective-permute-done((f32[2,2,64,3,128]{4,2,1,3,0:T(8,128)S(1)}, f32[2,2,64,3,128]{4,2,1,3,0:T(8,128)S(1)}, u32[]{:S(2)}, u32[]{:S(2)}) %collective-permute-start.4) | collective-permute-done | bytes 393248 | tf_op jit(solution)/shard_map/ppermute | solution.py:23
  153.6 0.4 pad_maximum_fusion.3
  153.9 1.8 subtract_add_fusion
  155.7 2.0 multiply_subtract_fusion
  157.8 0.6 convolution_bitcast_fusion
  158.3 0.6 convolution_bitcast_fusion.2
  158.9 2.2 fusion.36
  161.1 2.4 fusion
  163.5 0.6 fusion.13
  164.0 0.1 copy.64
  164.1 0.6 fusion.11
  164.7 0.1 copy.63
  164.8 0.5 fusion.89
  165.4 0.5 fusion.91
  165.9 0.8 fusion.9
  166.7 0.5 fusion.8
  167.2 0.8 pad_maximum_fusion.4
  168.1 0.0 all-reduce.5.cloned.1.call-start
  168.2 2.2 fusion.40
  170.4 427.3 %all-reduce.3.cloned.1.call-done = f32[2,8,64,64]{3,1,2,0:T(8,128)} async-done(((f32[2,8,64,64]{3,1,2,0:T(8,128)}), f32[2,8,64,64]{3,1,2,0:T(8,128)}) %all-reduce.3.cloned.1.call-update) | async-done | bytes 262160 | tf_op jit(solution)/shard_map/psum | solution.py:132
  597.7 0.0 all-reduce.5.cloned.1.call-update
  597.7 0.0 reduce-scatter.2.cloned.1.call-start
  597.8 2.2 fusion.1
  600.0 0.5 pad_maximum_fusion
  600.6 1.5 copy.60
  602.1 74.4 %all-reduce.5.cloned.1.call-done = f32[2,8,64,64]{3,1,2,0:T(8,128)} async-done(((f32[2,8,64,64]{3,1,2,0:T(8,128)}), f32[2,8,64,64]{3,1,2,0:T(8,128)}) %all-reduce.5.cloned.1.call-update) | async-done | bytes 262160 | tf_op jit(solution)/shard_map/psum | solution.py:132
  676.5 1.9 copy.67
  678.4 41.3 %reduce-scatter.2.cloned.1.call-done = f32[8,4,2,8,128]{4,3,2,1,0:T(8,128)} async-done(((f32[64,4,2,8,128]{4,3,2,1,0:T(8,128)}), f32[8,4,2,8,128]{4,3,2,1,0:T(8,128)}) %reduce-scatter.2.cloned.1.call-update) | async-done | bytes 262160 | tf_op jit(solution)/shard_map/reduce_scatter | solution.py:122
  (19 shorter events, 0.3 us)
Async XLA Ops:
  7.2 590.5 %all-reduce.3.cloned.1.call-start = ((), (), s32[]{:S(2)}) async-start(), calls=%async_computation.2 | async-start | bytes 1048576 | tf_op jit(solution)/shard_map/psum | solution.py:132
  7.2 20.3 %copy-start.1 = (f32[2,64,8,128]{3,2,1,0:T(8,128)S(1)}, f32[2,64,8,128]{3,2,1,0:T(8,128)}, u32[]{:S(2)}) copy-start(f32[2,64,8,128]{3,2,1,0:T(8,128)} %param.4) | copy-start | bytes 1572868
  7.2 20.3 %copy-start.3 = (f32[8,128]{1,0:T(8,128)S(1)}, f32[8,128]{1,0:T(8,128)}, u32[]{:S(2)}) copy-start(f32[8,128]{1,0:T(8,128)} %param.5) | copy-start | bytes 12292
  27.8 13.8 %copy-start = (f32[2,8,128,128]{3,2,1,0:T(8,128)S(1)}, f32[2,8,128,128]{3,2,1,0:T(8,128)}, u32[]{:S(2)}) copy-start(f32[2,8,128,128]{3,2,1,0:T(8,128)} %param.6) | copy-start | bytes 3145732
  28.1 14.9 %copy-start.2 = (f32[2,6,8,128]{3,2,1,0:T(8,128)S(1)}, f32[2,6,8,128]{3,2,1,0:T(8,128)}, u32[]{:S(2)}) copy-start(f32[2,6,8,128]{3,2,1,0:T(8,128)} %param.7) | copy-start | bytes 147460
  28.1 23.3 %collective-permute-start.1 = (f32[2,2,64,3,128]{4,2,1,3,0:T(8,128)S(1)}, f32[2,2,64,3,128]{4,2,1,3,0:T(8,128)S(1)}, u32[]{:S(2)}, u32[]{:S(2)}) collective-permute-start(f32[2,2,64,3,128]{4,2,1,3,0:T(8,128)S(1)} %get-tuple-element.24), channel_id=1, source_target_pairs={{1,0},{2,1},{3,2},{4,3},{5,4},{6,5},{7,6},{8,7},{9,8},{10,9},{11,1... | collective-permute-start | bytes 1179656 | tf_op jit(solution)/shard_map/ppermute | solution.py:25
  39.7 33.0 %collective-permute-start = (f32[2,2,64,3,128]{4,2,1,3,0:T(8,128)S(1)}, f32[2,2,64,3,128]{4,2,1,3,0:T(8,128)S(1)}, u32[]{:S(2)}, u32[]{:S(2)}) collective-permute-start(f32[2,2,64,3,128]{4,2,1,3,0:T(8,128)S(1)} %get-tuple-element.25), channel_id=1, source_target_pairs={{0,1},{1,2},{2,3},{3,4},{4,5},{5,6},{6,7},{7,8},{8,9},{9,10},{10,1... | collective-permute-start | bytes 1179656 | tf_op jit(solution)/shard_map/ppermute | solution.py:23
  77.3 26.2 %collective-permute-start.3 = (f32[2,2,64,3,128]{4,2,1,3,0:T(8,128)S(1)}, f32[2,2,64,3,128]{4,2,1,3,0:T(8,128)S(1)}, u32[]{:S(2)}, u32[]{:S(2)}) collective-permute-start(f32[2,2,64,3,128]{4,2,1,3,0:T(8,128)S(1)} %get-tuple-element.20), channel_id=1, source_target_pairs={{1,0},{2,1},{3,2},{4,3},{5,4},{6,5},{7,6},{8,7},{9,8},{10,9},{11,1... | collective-permute-start | bytes 1179656 | tf_op jit(solution)/shard_map/ppermute | solution.py:25
  86.2 25.4 %collective-permute-start.2 = (f32[2,2,64,3,128]{4,2,1,3,0:T(8,128)S(1)}, f32[2,2,64,3,128]{4,2,1,3,0:T(8,128)S(1)}, u32[]{:S(2)}, u32[]{:S(2)}) collective-permute-start(f32[2,2,64,3,128]{4,2,1,3,0:T(8,128)S(1)} %get-tuple-element.21), channel_id=1, source_target_pairs={{0,1},{1,2},{2,3},{3,4},{4,5},{5,6},{6,7},{7,8},{8,9},{9,10},{10,1... | collective-permute-start | bytes 1179656 | tf_op jit(solution)/shard_map/ppermute | solution.py:23
  115.9 15.0 %collective-permute-start.5 = (f32[2,2,64,3,128]{4,2,1,3,0:T(8,128)S(1)}, f32[2,2,64,3,128]{4,2,1,3,0:T(8,128)S(1)}, u32[]{:S(2)}, u32[]{:S(2)}) collective-permute-start(f32[2,2,64,3,128]{4,2,1,3,0:T(8,128)S(1)} %get-tuple-element.16), channel_id=1, source_target_pairs={{1,0},{2,1},{3,2},{4,3},{5,4},{6,5},{7,6},{8,7},{9,8},{10,9},{11,1... | collective-permute-start | bytes 1179656 | tf_op jit(solution)/shard_map/ppermute | solution.py:25
  123.3 30.2 %collective-permute-start.4 = (f32[2,2,64,3,128]{4,2,1,3,0:T(8,128)S(1)}, f32[2,2,64,3,128]{4,2,1,3,0:T(8,128)S(1)}, u32[]{:S(2)}, u32[]{:S(2)}) collective-permute-start(f32[2,2,64,3,128]{4,2,1,3,0:T(8,128)S(1)} %get-tuple-element.17), channel_id=1, source_target_pairs={{0,1},{1,2},{2,3},{3,4},{4,5},{5,6},{6,7},{7,8},{8,9},{9,10},{10,1... | collective-permute-start | bytes 1179656 | tf_op jit(solution)/shard_map/ppermute | solution.py:23
  168.1 508.4 %all-reduce.5.cloned.1.call-start = ((), (), s32[]{:S(2)}) async-start(), calls=%async_computation.3 | async-start | bytes 1048576 | tf_op jit(solution)/shard_map/psum | solution.py:132
  597.7 122.0 %reduce-scatter.2.cloned.1.call-start = ((), (), s32[]{:S(2)}) async-start(), calls=%async_computation.1 | async-start | bytes 2359296 | tf_op jit(solution)/shard_map/reduce_scatter | solution.py:122
Sparse Core Ops, SparseCore 0:
  168.2 429.4 all-reduce.2
  600.5 75.9 all-reduce.4
  679.6 40.0 reduce-scatter.1
